TPU v7x, 512 devices: a whole 4x4x16 slice. The times are simulated.
512 devices in a mesh: wide: 32 (over z, x_lo), narrow: 16 (over x_hi, y, core).
Axes of the slice: x: 4 (x_hi: 2, x_lo: 2; x = x_hi * 2 + x_lo), y: 4, z: 16, core: 2. Of those that a mesh axis runs over, the one named last changes fastest.
Arguments:
- queries: bfloat16 [256, 64, 128], P(None, 'narrow'), may hold values from -6 to 6
- shared_prefix_keys: bfloat16 [8192, 8, 128], P('wide'), may hold values from -6 to 6
- shared_prefix_values: bfloat16 [8192, 8, 128], P('wide'), may hold values from -6 to 6
- tenant_keys: bfloat16 [256, 8, 128], P('wide'), may hold values from -6 to 6
- tenant_values: bfloat16 [256, 8, 128], P('wide'), may hold values from -6 to 6
- attention_output_weight: bfloat16 [8192, 8192], P('narrow', 'wide'), may hold values from -0.125 to 0.125
- layer_residual_input: bfloat16 [256, 8192], P(None, 'wide'), may hold values from -2 to 2
- norm_gain_vector: bfloat16 [8192], P('wide'), may hold values from 0.099609375 to 1.8984375
- gate_matrix: bfloat16 [8192, 28672], P('wide', 'narrow'), may hold values from -0.0625 to 0.0625
- up_matrix: bfloat16 [8192, 28672], P('wide', 'narrow'), may hold values from -0.03125 to 0.03125
- adapter_down_factors: bfloat16 [64, 8192, 128], P('narrow', 'wide'), may hold values from -0.0625 to 0.0625
- adapter_up_factors: bfloat16 [64, 2, 64, 28672], P('wide', None, None, 'narrow'), may hold values from -0.1875 to 0.1875
- tenant_live_length: int32 [16], replicated, may hold values from 1 to 16, 192 in all
- tenant_adapter_index: int32 [16], replicated, may hold values from 0 to 63
- adapter_pool_row: int32 [64], replicated, may hold values from 0 to 63, each once
Outputs:
- stream_out: bfloat16 [256, 8192], P(None, 'wide')
- hidden: bfloat16 [256, 28672], P('wide', 'narrow')
Inputs may be any that keep to these rules, and one draw needn't show every extreme that they name: `tenant_live_length`: each tenant has 1 to 16 live rows, 192 in all, and some tenant fills all 16. `adapter_pool_row`: each pool row holds exactly one adapter.
All inputs are finite; a program needn't handle non-finite values.
Results may differ from a plain program's by a relative error of at most 0.025.
Values may be sent and summed in bfloat16 or wider, within the bound.
A program may use at most 128 MiB of HBM per device.

v0:
```python
import jax
import jax.numpy as jnp
from jax import lax
from jax.sharding import PartitionSpec as P

MODEL_WIDTH = 8192
QH = 64
KVH = 8
ADAPTER_RANK = 64
TENANTS = 16
ROWS_T = 16


def row_tables(tenant_live_length, tenant_adapter_index, adapter_pool_row):
    pool_ids = jnp.arange(adapter_pool_row.shape[0], dtype=jnp.int32)
    tenant_pool_slot = jnp.sum(
        jnp.where(tenant_adapter_index[:, None] == pool_ids[None, :], adapter_pool_row[None, :], 0),
        axis=1,
    )
    row_ids = jnp.arange(TENANTS * ROWS_T, dtype=jnp.int32)
    tenant_of = row_ids // ROWS_T
    position = row_ids % ROWS_T
    chosen = tenant_of[:, None] == jnp.arange(TENANTS, dtype=jnp.int32)[None, :]
    row_length = jnp.sum(jnp.where(chosen, tenant_live_length[None, :], 0), axis=1)
    row_adapter_slot = jnp.sum(jnp.where(chosen, tenant_pool_slot[None, :], 0), axis=1)
    return (tenant_of, position, position < row_length, tenant_pool_slot, row_adapter_slot)


def build_adapter_terms(
    normed_rows,
    lowrank_rows,
    row_adapter_slot,
    tenant_row_ids,
    gate_matrix,
    up_matrix,
    adapter_up_factors,
):

    def hidden_terms(start, count):
        owned = row_adapter_slot[None, :] == tenant_row_ids[:, None]
        masked_scores = jnp.where(
            owned[:, :, None, None], lowrank_rows[None], jnp.zeros((), jnp.bfloat16)
        )
        adapter_update = jnp.einsum(
            "ljze,lzep->jzp", masked_scores, adapter_up_factors, preferred_element_type=jnp.float32
        )
        gate_part = (
            jnp.dot(normed_rows, gate_matrix, preferred_element_type=jnp.float32)
            + adapter_update[:, 0]
        )
        up_part = (
            jnp.dot(normed_rows, up_matrix, preferred_element_type=jnp.float32)
            + adapter_update[:, 1]
        )
        return jnp.concatenate([gate_part, up_part], axis=1)

    return hidden_terms


def body(
    queries,
    shared_prefix_keys,
    shared_prefix_values,
    tenant_keys,
    tenant_values,
    attention_output_weight,
    layer_residual_input,
    norm_gain_vector,
    gate_matrix,
    up_matrix,
    adapter_down_factors,
    adapter_up_factors,
    tenant_live_length,
    tenant_adapter_index,
    adapter_pool_row,
):
    tenant_of, position, live, tenant_pool_slot, row_adapter_slot = row_tables(
        tenant_live_length, tenant_adapter_index, adapter_pool_row
    )
    rows = queries.shape[0]
    heads_here = queries.shape[1]
    head_size = queries.shape[2]
    group = QH // KVH
    kv_here = max(1, heads_here // group)
    per_kv = heads_here // kv_here
    wide_at = lax.axis_index("wide")
    narrow_at = lax.axis_index("narrow")
    kv_start = narrow_at * heads_here // group
    keys_here = lax.dynamic_slice_in_dim(shared_prefix_keys, kv_start, kv_here, 1)
    values_here = lax.dynamic_slice_in_dim(shared_prefix_values, kv_start, kv_here, 1)
    near_keys = lax.dynamic_slice_in_dim(tenant_keys, kv_start, kv_here, 1)
    near_values = lax.dynamic_slice_in_dim(tenant_values, kv_start, kv_here, 1)
    own_rows = tenant_keys.shape[0]
    key_ids = wide_at * own_rows + jnp.arange(own_rows, dtype=jnp.int32)
    key_live = lax.dynamic_slice_in_dim(live, wide_at * own_rows, own_rows, 0)
    allowed = (
        (tenant_of[:, None] == (key_ids // ROWS_T)[None, :])
        & ((key_ids % ROWS_T)[None, :] <= position[:, None])
        & key_live[None, :]
    )
    mask_four = allowed[:, None, None, :]
    scale = head_size ** (-0.5)
    grouped = queries.reshape(rows, kv_here, per_kv, head_size)
    far = (
        jnp.einsum("rkgd,jkd->rkgj", grouped, keys_here, preferred_element_type=jnp.float32) * scale
    )
    near = (
        jnp.einsum("rkgd,jkd->rkgj", grouped, near_keys, preferred_element_type=jnp.float32) * scale
    )
    near = jnp.where(mask_four, near, -jnp.inf)
    top = jnp.maximum(jnp.max(far, axis=3), jnp.max(near, axis=3))
    far_w = jnp.exp(far - top[..., None])
    near_w = jnp.where(mask_four, jnp.exp(near - top[..., None]), 0.0)
    total = jnp.sum(far_w, axis=3) + jnp.sum(near_w, axis=3)
    summed = jnp.einsum(
        "rkgj,jkd->rkgd",
        far_w.astype(jnp.bfloat16),
        values_here,
        preferred_element_type=jnp.float32,
    )
    summed = summed + jnp.einsum(
        "rkgj,jkd->rkgd",
        near_w.astype(jnp.bfloat16),
        near_values,
        preferred_element_type=jnp.float32,
    )
    top = top.reshape(rows, heads_here)
    total = total.reshape(rows, heads_here)
    summed = summed.reshape(rows, heads_here, head_size)
    highest = lax.pmax(top, "wide")
    factor = jnp.exp(top - highest)
    total, summed = lax.psum((total * factor, summed * factor[..., None]), "wide")
    attended = (
        (summed / total[..., None]).astype(jnp.bfloat16).reshape(rows, heads_here * head_size)
    )
    projected = lax.psum(
        jnp.dot(attended, attention_output_weight, preferred_element_type=jnp.float32), "narrow"
    )
    stream_out = jnp.where(
        live[:, None], layer_residual_input.astype(jnp.float32) + projected, 0.0
    ).astype(jnp.bfloat16)
    stream_f = stream_out.astype(jnp.float32)
    squares = lax.psum(jnp.sum(stream_f * stream_f, axis=1), "wide")
    normed_rows = (
        stream_f
        * lax.rsqrt(squares / MODEL_WIDTH + 1e-05)[:, None]
        * norm_gain_vector.astype(jnp.float32)[None, :]
    ).astype(jnp.bfloat16)
    partial_result = lax.all_gather(adapter_down_factors, "narrow", axis=0, tiled=True)
    pool_ids = jnp.arange(partial_result.shape[0], dtype=jnp.int32)
    selector = (tenant_pool_slot[:, None] == pool_ids[None, :]).astype(jnp.bfloat16)
    down_factor = jnp.einsum(
        "tk,kdr->tdr", selector, partial_result, preferred_element_type=jnp.float32
    ).astype(jnp.bfloat16)
    partial_low = jnp.einsum(
        "tsd,tdk->tsk",
        normed_rows.reshape(TENANTS, ROWS_T, normed_rows.shape[1]),
        down_factor,
        preferred_element_type=jnp.float32,
    ).reshape(rows, down_factor.shape[2])
    lowrank_rows = lax.psum(partial_low, "wide").astype(jnp.bfloat16).reshape(rows, 2, ADAPTER_RANK)
    whole_pool_terms = adapter_up_factors.shape[0]
    width_here = gate_matrix.shape[1]
    tenant_row_ids = wide_at * whole_pool_terms + jnp.arange(whole_pool_terms, dtype=jnp.int32)
    wide_count = lax.axis_size("wide")
    adapter_terms = build_adapter_terms(
        normed_rows,
        lowrank_rows,
        row_adapter_slot,
        tenant_row_ids,
        gate_matrix,
        up_matrix,
        adapter_up_factors,
    )
    sums = lax.psum_scatter(
        adapter_terms(jnp.int32(0), rows // wide_count * lax.axis_size("wide")),
        "wide",
        scatter_dimension=0,
        tiled=True,
    )
    hidden = (jax.nn.silu(sums[:, :width_here]) * sums[:, width_here:]).astype(jnp.bfloat16)
    return (stream_out, hidden)


def solution(mesh):
    in_specs = (
        P(None, "narrow", None),
        P("wide", None, None),
        P("wide", None, None),
        P("wide", None, None),
        P("wide", None, None),
        P("narrow", "wide"),
        P(None, "wide"),
        P("wide"),
        P("wide", "narrow"),
        P("wide", "narrow"),
        P("narrow", "wide", None),
        P("wide", None, None, "narrow"),
        P(),
        P(),
        P(),
    )
    out_specs = (P(None, "wide"), P("wide", "narrow"))
    return jax.shard_map(body, mesh=mesh, in_specs=in_specs, out_specs=out_specs, check_vma=False)
```

profile of v0, /device:TPU:16, one launch (start us, length us, event | category | flops | bytes accessed | tf_op | source)
XLA Modules:
  0.0 853.3 jit_solution(16533834852076110561)
XLA Ops:
  7.2 0.0 copy-start
  7.2 0.0 all-reduce.4.cloned.1.call-start
  7.3 0.9 select_reduce_fusion.2
  8.2 0.7 select_reduce_fusion
  8.9 0.7 constant_dynamic-slice_fusion.1
  9.7 0.7 constant_dynamic-slice_fusion
  10.4 1.5 constant_dynamic-slice_fusion.2
  11.9 0.0 copy-start.4
  11.9 0.1 copy.43
  12.0 0.1 dynamic_slice.17
  12.1 1.3 fusion.44
  13.4 0.0 copy-start.6
  13.4 0.0 copy-start.5
  13.4 0.1 and_and_fusion
  13.5 1.1 fusion.45
  14.6 70.4 %pmax.7 = f32[256,4]{0,1:T(4,128)S(1)} all-reduce(f32[256,4]{0,1:T(4,128)S(1)} %max.12), channel_id=1, replica_groups=mesh['wide'=32,'narrow'=16] {'wide'}, use_global_device_ids=true, to_apply=%region_3.4 | all-reduce | flops 1024 | bytes 8192 | tf_op jit(solution)/shard_map/pmax | solution.py:130
  85.0 0.2 fusion.12
  85.2 0.3 fusion.16
  85.5 1.1 fusion.7
  86.6 0.0 all-reduce.4.cloned.1.call-update
  86.6 0.0 all-reduce.6.cloned.1.call-start
  86.7 60.0 %psum.36 = f32[256,4]{0,1:T(4,128)S(1)} all-reduce(f32[256,4]{0,1:T(4,128)S(1)} %get-tuple-element.6), channel_id=1, replica_groups=mesh['wide'=32,'narrow'=16] {'wide'}, use_global_device_ids=true, to_apply=%region_7.8 | all-reduce | flops 1024 | bytes 8192 | tf_op jit(solution)/shard_map/psum | solution.py:132
  146.7 198.3 %all-reduce.4.cloned.1.call-done = f32[256,4,128]{0,2,1:T(8,128)} async-done(((f32[256,4,128]{0,2,1:T(8,128)}), f32[256,4,128]{0,2,1:T(8,128)}) %all-reduce.4.cloned.1.call-update) | async-done | bytes 524304 | tf_op jit(solution)/shard_map/psum | solution.py:132
  345.0 1.1 divide_convert_fusion
  346.0 0.0 copy-done.4
  346.1 1.0 fusion.46
  347.0 0.0 all-reduce.6.cloned.1.call-update
  347.1 0.0 all-gather.2.cloned.1.call-start
  347.1 0.7 all-gather.2.cloned.1.call-update
  347.8 0.0 reduce-scatter.2.cloned.1.call-start
  347.8 0.0 copy-done.6
  347.9 0.1 broadcast_compare_fusion
  348.0 145.1 %all-reduce.6.cloned.1.call-done = f32[256,256]{1,0:T(8,128)} async-done(((f32[256,256]{1,0:T(8,128)}), f32[256,256]{1,0:T(8,128)}) %all-reduce.6.cloned.1.call-update) | async-done | bytes 262160 | tf_op jit(solution)/shard_map/psum | solution.py:136
  493.0 0.0 copy-done.5
  493.0 1.1 fusion.19
  494.2 0.0 copy-start.3
  494.2 64.1 %psum.38 = f32[256]{0:T(256)S(1)} all-reduce(f32[256]{0:T(256)S(1)} %get-tuple-element.4), channel_id=1, replica_groups=mesh['wide'=32,'narrow'=16] {'wide'}, use_global_device_ids=true, to_apply=%region_10.11 | all-reduce | flops 256 | bytes 2048 | tf_op jit(solution)/shard_map/psum | solution.py:143
  558.3 0.1 fusion.21
  558.4 14.9 %all-gather.2.cloned.1.call-done = bf16[64,256,128]{2,1,0:T(8,128)(2,1)} async-done(((bf16[4,256,128]{2,1,0:T(8,128)(2,1)}), bf16[64,256,128]{2,1,0:T(8,128)(2,1)}) %all-gather.2.cloned.1.call-update) | async-done | bytes 4194320 | tf_op jit(solution)/shard_map/all_gather | solution.py:149
  573.3 4.6 fusion.2
  578.0 0.0 copy-start.1
  578.0 0.3 fusion.10
  578.3 0.1 copy.52
  578.4 122.3 %all-reduce.7 = bf16[256,128]{0,1:T(8,128)(2,1)S(1)} all-reduce(f32[256,128]{0,1:T(8,128)S(1)} %copy.52), channel_id=1, replica_groups=mesh['wide'=32,'narrow'=16] {'wide'}, use_global_device_ids=true, to_apply=%region_13.14 | all-reduce | flops 32768 | bytes 196608 | tf_op jit(solution)/shard_map/psum | solution.py:161
  700.7 0.0 copy-done
  700.7 0.0 copy-start.2
  700.7 0.7 convolution_bitcast_fusion
  701.4 0.0 copy-done.3
  701.4 0.0 copy-done.1
  701.4 0.4 convolution_add_fusion
  701.8 0.1 copy-done.2
  701.9 0.4 convolution_add_fusion.1
  702.3 2.3 pad_maximum_fusion
  704.6 0.0 reduce-scatter.2.cloned.1.call-update
  704.6 140.6 %reduce-scatter.2.cloned.1.call-done = f32[8,3584]{1,0:T(8,128)} async-done(((f32[256,3584]{1,0:T(8,128)}), f32[8,3584]{1,0:T(8,128)}) %reduce-scatter.2.cloned.1.call-update) | async-done | bytes 114704 | tf_op jit(solution)/shard_map/reduce_scatter | solution.py:175
  845.2 1.5 fusion.29
  (9 shorter events, 0.1 us)
Async XLA Ops:
  7.2 693.6 %copy-start = (bf16[2,2,64,1792]{3,2,1,0:T(8,128)(2,1)S(1)}, bf16[2,2,64,1792]{3,2,1,0:T(8,128)(2,1)}, u32[]{:S(2)}) copy-start(bf16[2,2,64,1792]{3,2,1,0:T(8,128)(2,1)} %param.26) | copy-start | bytes 2752516
  7.2 337.8 %all-reduce.4.cloned.1.call-start = ((), (), s32[]{:S(2)}) async-start(), calls=%async_computation.1 | async-start | bytes 1048576 | tf_op jit(solution)/shard_map/psum | solution.py:132
  11.9 334.2 %copy-start.4 = (bf16[512,256]{1,0:T(8,128)(2,1)S(1)}, bf16[512,256]{1,0:T(8,128)(2,1)}, u32[]{:S(2)}) copy-start(bf16[512,256]{1,0:T(8,128)(2,1)} %param.20) | copy-start | bytes 786436
  13.4 334.5 %copy-start.6 = (bf16[256]{0:T(256)(128)(2,1)S(1)}, bf16[256]{0:T(256)(128)(2,1)}, u32[]{:S(2)}) copy-start(bf16[256]{0:T(256)(128)(2,1)} %param.22) | copy-start | bytes 1540
  13.4 479.7 %copy-start.5 = (bf16[256,256]{1,0:T(8,128)(2,1)S(1)}, bf16[256,256]{1,0:T(8,128)(2,1)}, u32[]{:S(2)}) copy-start(bf16[256,256]{1,0:T(8,128)(2,1)} %param.21) | copy-start | bytes 393220
  86.6 406.4 %all-reduce.6.cloned.1.call-start = ((), (), s32[]{:S(2)}) async-start(), calls=%async_computation.2 | async-start | bytes 524288 | tf_op jit(solution)/shard_map/psum | solution.py:136
  347.1 226.3 %all-gather.2.cloned.1.call-start = ((), (), s32[]{:S(2)}) async-start(), calls=%async_computation.3 | async-start | bytes 4456448 | tf_op jit(solution)/shard_map/all_gather | solution.py:149
  347.8 497.4 %reduce-scatter.2.cloned.1.call-start = ((), (), s32[]{:S(2)}) async-start(), calls=%async_computation.4 | async-start | bytes 3784704 | tf_op jit(solution)/shard_map/reduce_scatter | solution.py:175
  494.2 207.2 %copy-start.3 = (bf16[256,256]{1,0:T(8,128)(2,1)}, bf16[256,256]{1,0:T(8,128)(2,1)S(1)}, u32[]{:S(2)}) copy-start(bf16[256,256]{1,0:T(8,128)(2,1)S(1)} %get-tuple-element.5) | copy-start | bytes 393220
  578.0 123.5 %copy-start.1 = (bf16[256,1792]{1,0:T(8,128)(2,1)S(1)}, bf16[256,1792]{1,0:T(8,128)(2,1)}, u32[]{:S(2)}) copy-start(bf16[256,1792]{1,0:T(8,128)(2,1)} %param.24) | copy-start | bytes 2752516
  700.7 1.2 copy-start.2
Sparse Core Ops, SparseCore 0:
  86.7 258.1 all-reduce.3
  348.1 144.8 all-reduce.5
  496.4 76.9 all-gather.1
  704.7 140.4 reduce-scatter.1
where the time goes:
time: 854 us; the launch traced here: 853 us
  waiting for transfers between devices  500 us (59%)
  blocking collectives  317 us (37%)
  between operations  14 us (2%)
  matrix products  11.2 us (1%)
    psum x1, waiting for transfers between devices, body(): lax.psum((total * factor, summed * factor[..., None]), 'wide')  198 us
    psum x1, waiting for transfers between devices, body(): lax.psum(jnp.dot(attended, attention_output_weight, preferred_element_typ...  145 us
    reduce_scatter x1, waiting for transfers between devices, body(): lax.psum_scatter(adapter_terms(jnp.int32(0), rows // wide_count * lax.axi...  141 us
    psum x1, blocking collectives, body(): lax.psum(partial_low, 'wide').astype(jnp.bfloat16)  122 us
    pmax x1, blocking collectives, body(): highest = lax.pmax(top, 'wide')  70.4 us
    psum x1, blocking collectives, body(): squares = lax.psum(jnp.sum(stream_f * stream_f, axis=1), 'wide')  64.1 us
    psum x1, blocking collectives, body(): lax.psum((total * factor, summed * factor[..., None]), 'wide')  60 us
  transfers between devices with their start and end apart: 4, of which 4 were waited for; matrix products, arithmetic and copies ran while one was open for 0% of the time, Pallas kernels for 0%

commit v1 on v0

v1 whole, which is shorter than its diff:
```python
import functools

import jax
import jax.numpy as jnp
from jax import lax
from jax.experimental import pallas as pl
from jax.experimental.pallas import tpu as pltpu
from jax.sharding import PartitionSpec as P

MODEL_WIDTH = 8192
RANK = 64
TENANTS = 16
ROWS_T = 16
ROWS = 256
HD = 128
ZS = 16
NS = 16
NEAR = 16
MESH = pl.DeviceIdType.MESH
F32 = jnp.float32
BF16 = jnp.bfloat16


def dot(a, b):
    return jnp.dot(a, b, preferred_element_type=F32)


def dot_t(a, b):
    return lax.dot_general(a, b, (((1,), (1,)), ((), ())), preferred_element_type=F32)


def kernel(
    lens, tai, pool, q, kv, wo, resid, gain, gate, up, down, upf,
    stream_out, hidden_out,
    kvp, wbuf, rbuf, gbuf, ubuf, fbuf, down8, dsend, drecv,
    obuf, lse_s, arecv, lrecv, lt, attbuf, cbuf, crecv, sbuf,
    low_z, low_p, ss_s, ss_r, sst, ss_x, ss_y, pg, pu,
    dn_s, dn_r, up_s, up_r, xs, xr,
    loc_sem, one_s, one_r, d_s, d_r, a_s, a_r, l_s, l_r, b_s, b_r, c_s, c_r,
    e_s, e_r, lz_s, lz_r, lp_s, lp_r, q_s, q_r,
    dns_sem, dnr_sem, ups_sem, upr_sem, x_s, x_r,
):
    w = lax.axis_index("wide")
    n = lax.axis_index("narrow")
    z, x = lax.div(w, 2), lax.rem(w, 2)
    chip, core = lax.div(n, 2), lax.rem(n, 2)
    ox = 1 - x
    width = gate.shape[1]
    half = width // 2

    def zdev(j):
        return (j * 2 + x, n)

    def pdev(j):
        return (z * 2 + lax.div(j, NS), lax.rem(j, NS))

    me_p = x * NS + n
    x_dev = (z * 2 + ox, n)
    core_dev = (w, chip * 2 + 1 - core)

    def remote(src, dst, ss, rs, dev):
        return pltpu.make_async_remote_copy(
            src_ref=src, dst_ref=dst, send_sem=ss, recv_sem=rs, device_id=dev, device_id_type=MESH
        )

    def loop(lo, hi, fn):
        def step(i, carry):
            fn(i)
            return carry

        lax.fori_loop(lo, hi, step, 0)

    local = [
        pltpu.make_async_copy(wo.at[pl.ds(pl.multiple_of(x * 256, 256), 256)], wbuf.at[x], loc_sem.at[0]),
        pltpu.make_async_copy(resid.at[pl.ds(pl.multiple_of(n * 16, 16), 16)], rbuf, loc_sem.at[1]),
        pltpu.make_async_copy(down, down8.at[pl.ds(pl.multiple_of(core * 4, 4), 4)], loc_sem.at[2]),
        pltpu.make_async_copy(gate, gbuf, loc_sem.at[3]),
        pltpu.make_async_copy(up, ubuf, loc_sem.at[4]),
        pltpu.make_async_copy(upf, fbuf, loc_sem.at[5]),
    ]
    for c in local:
        c.start()

    barrier = pltpu.get_barrier_semaphore()

    def greet_z(k):
        pl.semaphore_signal(barrier, inc=1, device_id=zdev(lax.rem(z + k, ZS)), device_id_type=MESH)

    def greet_p(k):
        pl.semaphore_signal(barrier, inc=1, device_id=pdev(lax.rem(me_p + k, 32)), device_id_type=MESH)

    loop(1, ZS, greet_z)
    loop(1, 32, greet_p)
    pl.semaphore_wait(barrier, ZS - 1 + 31)

    kv_copy = remote(kv, kvp, one_s.at[0], one_r.at[0], x_dev)
    kv_copy.start()
    down_copy = remote(
        down, down8.at[pl.ds(pl.multiple_of(core * 4, 4), 4)], one_s.at[1], one_r.at[1], core_dev
    )
    down_copy.start()
    wo_copy = remote(
        wo.at[pl.ds(pl.multiple_of(ox * 256, 256), 256)], wbuf.at[x], one_s.at[2], one_r.at[2], x_dev
    )
    wo_copy.start()

    slots = [pool[tai[t]] for t in range(TENANTS)]

    scale = HD ** (-0.5)
    qv = q[...]
    s_a = dot_t(qv, kv[0, :256]) * scale

    local[2].wait()
    down_copy.wait()

    def pick(i):
        slot = pool[tai[2 * i + core]]
        block = down8[lax.rem(slot, 8)]
        mine = lax.div(slot, 8) == chip
        dsend[i] = jnp.where(mine, block, jnp.zeros_like(block))

    loop(0, 8, pick)

    def send_down(k):
        j = lax.rem(chip + k, 8)
        remote(dsend.at[j], drecv.at[chip], d_s.at[j], d_r.at[chip], (w, j * 2 + core)).start()

    loop(1, 8, send_down)

    kv_copy.wait()
    s_b = dot_t(qv, kvp[0, :256]) * scale
    m = jnp.maximum(jnp.max(s_a, axis=1, keepdims=True), jnp.max(s_b, axis=1, keepdims=True))
    p_a = jnp.exp(s_a - m)
    p_b = jnp.exp(s_b - m)
    l = jnp.sum(p_a, axis=1, keepdims=True) + jnp.sum(p_b, axis=1, keepdims=True)
    o = dot(p_a.astype(BF16), kv[1, :256]) + dot(p_b.astype(BF16), kvp[1, :256])
    o = o / l
    lse = m + jnp.log(l)
    obuf[...] = o.astype(BF16).reshape(ZS, 32, HD)
    lse_rows = jnp.transpose(jnp.broadcast_to(lse, (512, 128)))
    for i in range(4):
        lse_s[i] = lse_rows[0:1, 128 * i : 128 * i + 128]

    def send_a(k):
        j = lax.rem(z + k, ZS)
        remote(obuf.at[j], arecv.at[z], a_s.at[j], a_r.at[z], zdev(j)).start()
        remote(lse_s.at[lax.div(j, 4)], lrecv.at[z], l_s.at[j], l_r.at[z], zdev(j)).start()

    loop(1, ZS, send_a)
    arecv[z] = obuf[z]
    lrecv[z] = lse_s[lax.div(z, 4)]

    nk = kv[0, 256:272] + kvp[0, 256:272]
    nv = kv[1, 256:272] + kvp[1, 256:272]
    q_own = q[pl.ds(pl.multiple_of(z * 32, 32), 32), :]
    near = dot_t(q_own, nk) * scale
    row = lax.rem(lax.broadcasted_iota(jnp.int32, (32, NEAR), 0), ROWS_T)
    col = lax.broadcasted_iota(jnp.int32, (32, NEAR), 1)
    ok = (col <= row) & (col < lens[z])
    near = jnp.where(ok, near, -jnp.inf)
    m_n = jnp.max(near, axis=1, keepdims=True)
    p_n = jnp.where(ok, jnp.exp(near - m_n), 0.0)
    l_n = jnp.sum(p_n, axis=1, keepdims=True)
    o_n = dot(p_n.astype(BF16), nv) / l_n
    lse_n = m_n + jnp.log(l_n)

    drecv[chip] = dsend[chip]

    def wait_a(k):
        j = lax.rem(z + k, ZS)
        remote(lse_s.at[lax.div(j, 4)], lrecv.at[j], l_s.at[j], l_r.at[j], zdev(j)).wait()
        remote(obuf.at[j], arecv.at[j], a_s.at[j], a_r.at[j], zdev(j)).wait()

    loop(1, ZS, wait_a)
    rows16 = jnp.concatenate([lrecv[s] for s in range(ZS)], axis=0)
    lt[...] = jnp.transpose(jnp.concatenate([rows16] * 8, axis=0))
    cols = lt[pl.ds(pl.multiple_of(lax.rem(z, 4) * 32, 32), 32), :]
    top = jnp.maximum(jnp.max(cols, axis=1, keepdims=True), lse_n)
    part = jnp.exp(cols - top)
    w_n = jnp.exp(lse_n - top)
    lane = lax.broadcasted_iota(jnp.int32, (32, 128), 1)
    total = jnp.sum(jnp.where(lane < ZS, part, 0.0), axis=1, keepdims=True) + w_n
    acc = w_n * o_n
    for s in range(ZS):
        acc = acc + part[:, s : s + 1] * arecv[s].astype(F32)
    acc = acc / total
    attbuf[z] = jnp.concatenate([acc[:16], acc[16:]], axis=1).astype(BF16)

    def send_b(k):
        j = lax.rem(z + k, ZS)
        remote(attbuf.at[z], attbuf.at[z], b_s.at[j], b_r.at[z], zdev(j)).start()

    loop(1, ZS, send_b)
    local[0].wait()
    wo_copy.wait()

    def wait_d(k):
        j = lax.rem(chip + k, 8)
        remote(dsend.at[j], drecv.at[j], d_s.at[j], d_r.at[j], (w, j * 2 + core)).wait()

    def wait_b(k):
        j = lax.rem(z + k, ZS)
        remote(attbuf.at[z], attbuf.at[j], b_s.at[j], b_r.at[j], zdev(j)).wait()

    loop(1, ZS, wait_b)
    att = attbuf[...].reshape(ROWS, 256)
    for xf in range(2):
        cbuf[pl.ds(xf * NS, NS)] = dot(att, wbuf[xf]).astype(BF16).reshape(NS, 16, 256)

    def send_c(k):
        j = lax.rem(me_p + k, 32)
        remote(cbuf.at[j], crecv.at[me_p], c_s.at[j], c_r.at[me_p], pdev(j)).start()

    loop(1, 32, send_c)
    crecv[me_p] = cbuf[me_p]
    local[1].wait()
    loop(1, 8, wait_d)
    dsel = drecv[0].astype(F32)
    for i in range(1, 8):
        dsel = dsel + drecv[i].astype(F32)
    dsel = dsel.astype(BF16)

    def wait_c(k):
        j = lax.rem(me_p + k, 32)
        remote(cbuf.at[j], crecv.at[j], c_s.at[j], c_r.at[j], pdev(j)).wait()

    loop(1, 32, wait_c)
    acc = rbuf[...].astype(F32)
    for s in range(32):
        acc = acc + crecv[s].astype(F32)
    pos = lax.broadcasted_iota(jnp.int32, (16, 256), 0)
    mine = jnp.where(pos < lens[n], acc, 0.0).astype(BF16)
    sbuf[n] = mine

    def send_e(k):
        j = lax.rem(n + k, NS)
        remote(sbuf.at[n], sbuf.at[n], e_s.at[j], e_r.at[n], (w, j)).start()

    loop(1, NS, send_e)

    gain_row = gain[...]
    low = dot((mine.astype(F32) * gain_row).astype(BF16), dsel)
    low_z[z] = low.astype(BF16)

    def send_lz(k):
        j = lax.rem(z + k, ZS)
        remote(low_z.at[z], low_z.at[z], lz_s.at[j], lz_r.at[z], zdev(j)).start()

    loop(1, ZS, send_lz)

    def wait_e(k):
        j = lax.rem(n + k, NS)
        remote(sbuf.at[n], sbuf.at[j], e_s.at[j], e_r.at[j], (w, j)).wait()

    loop(1, NS, wait_e)
    stream = sbuf[...].reshape(ROWS, 256)
    stream_out[...] = stream
    sf = stream.astype(F32)
    y = (sf * gain_row).astype(BF16)
    local[3].wait()
    pg[...] = dot(y, gbuf[...])
    local[4].wait()
    pu[...] = dot(y, ubuf[...])

    ssq = jnp.sum(sf * sf, axis=1, keepdims=True)
    ss_rows = jnp.transpose(jnp.broadcast_to(ssq, (ROWS, 128)))
    for i in range(2):
        ss_s[i] = ss_rows[0:1, 128 * i : 128 * i + 128]

    def wait_lz(k):
        j = lax.rem(z + k, ZS)
        remote(low_z.at[z], low_z.at[j], lz_s.at[j], lz_r.at[j], zdev(j)).wait()

    loop(1, ZS, wait_lz)
    acc = low_z[0].astype(F32)
    for s in range(1, ZS):
        acc = acc + low_z[s].astype(F32)
    low_p[me_p] = acc.astype(BF16)

    def send_lp(k):
        j = lax.rem(me_p + k, 32)
        remote(low_p.at[me_p], low_p.at[me_p], lp_s.at[j], lp_r.at[me_p], pdev(j)).start()

    loop(1, 32, send_lp)

    def send_ss(k):
        j = lax.rem(z + k, ZS)
        remote(ss_s.at[lax.div(j, 8)], ss_r.at[z], q_s.at[j], q_r.at[z], zdev(j)).start()

    loop(1, ZS, send_ss)
    ss_r[z] = ss_s[lax.div(z, 8)]

    local[5].wait()
    smap = jnp.concatenate([jnp.full((ROWS_T, 128), slots[t], jnp.int32) for t in range(TENANTS)], axis=0)
    lane2 = lax.broadcasted_iota(jnp.int32, (ROWS, 128), 1)
    first = lane2 < RANK
    owned = smap == (2 * w + jnp.where(first, 0, 1))
    u_gate = jnp.concatenate([fbuf[0, 0], fbuf[1, 0]], axis=0)
    u_up = jnp.concatenate([fbuf[0, 1], fbuf[1, 1]], axis=0)

    def wait_lp(k):
        j = lax.rem(me_p + k, 32)
        remote(low_p.at[me_p], low_p.at[j], lp_s.at[j], lp_r.at[j], pdev(j)).wait()

    loop(1, 32, wait_lp)
    lows = low_p[...].astype(F32).reshape(2, ROWS, 128)
    lows = (lows[0] + lows[1]).astype(BF16).astype(F32)
    rolled = pltpu.roll(lows, RANK, 1)
    l_gate = jnp.where(owned, jnp.where(first, lows, rolled), 0.0).astype(BF16)
    l_up = jnp.where(owned, jnp.where(first, rolled, lows), 0.0).astype(BF16)
    pg[...] += dot(l_gate, u_gate)
    pu[...] += dot(l_up, u_up)

    below, above = lax.rem(z + ZS - 1, ZS), lax.rem(z + 1, ZS)
    parts = [(pg, 0), (pg, half), (pu, 0), (pu, half)]

    def own_rows(i, t):
        ref, at = parts[i]
        return ref[pl.ds(pl.multiple_of(t * 16, 16), 16), at : at + half]

    def dn_copy(s, i):
        return remote(dn_s.at[s, i], dn_r.at[s, i], dns_sem.at[s, i], dnr_sem.at[s, i], zdev(below))

    def up_copy(s, i):
        return remote(up_s.at[s, i], up_r.at[s, i], ups_sem.at[s, i], upr_sem.at[s, i], zdev(above))

    for i in range(4):
        dn_s[0, i] = own_rows(i, lax.rem(z + 8, ZS)).astype(BF16)
        dn_copy(0, i).start()
        up_s[0, i] = own_rows(i, lax.rem(z + 7, ZS)).astype(BF16)
        up_copy(0, i).start()

    def ring(s):
        for i in range(4):
            dn_copy(s - 1, i).wait_recv()
            got = dn_r[s - 1, i].astype(F32) + own_rows(i, lax.rem(z + 8 + s, ZS))
            dn_s[s, i] = got.astype(BF16)
            dn_copy(s, i).start()
            up_copy(s - 1, i).wait_recv()
            got = up_r[s - 1, i].astype(F32) + own_rows(i, lax.rem(z + 7 - s + ZS, ZS))
            up_s[s, i] = got.astype(BF16)
            up_copy(s, i).start()

    loop(1, 7, ring)
    for i in range(4):
        dn_copy(6, i).wait_recv()
        got = dn_r[6, i].astype(F32) + own_rows(i, lax.rem(z + 15, ZS))
        dn_s[7, i] = got.astype(BF16)
        dn_copy(7, i).start()

    def wait_ss(k):
        j = lax.rem(z + k, ZS)
        remote(ss_s.at[lax.div(j, 8)], ss_r.at[j], q_s.at[j], q_r.at[j], zdev(j)).wait()

    loop(1, ZS, wait_ss)
    acc = ss_r[0]
    for s in range(1, ZS):
        acc = acc + ss_r[s]
    ss_x[...] = acc
    ss_copy = remote(ss_x, ss_y, x_s.at[0], x_r.at[0], x_dev)
    ss_copy.start()

    sums = []
    for i in range(4):
        up_copy(6, i).wait_recv()
        part_sum = own_rows(i, z) + up_r[6, i].astype(F32)
        dn_copy(7, i).wait_recv()
        part_sum = part_sum + dn_r[7, i].astype(F32)
        other = jnp.where(x == 0, part_sum[8:], part_sum[:8])
        xs_rows = other
        sums.append(jnp.where(x == 0, part_sum[:8], part_sum[8:]))
        if i % 2 == 0:
            held = xs_rows
        else:
            xs[i // 2] = jnp.concatenate([held, xs_rows], axis=0).astype(BF16)
            remote(xs.at[i // 2], xr.at[i // 2], x_s.at[1 + i // 2], x_r.at[1 + i // 2], x_dev).start()

    ss_copy.wait()
    squares = ss_x[...] + ss_y[...]
    sst[...] = jnp.transpose(jnp.broadcast_to(squares, (128, 128)))
    own_sq = sst[pl.ds(pl.multiple_of(lax.rem(z, 8) * 16 + x * 8, 8), 8), 0:1]
    rs = lax.rsqrt(own_sq / MODEL_WIDTH + 1e-05)
    for i in range(2):
        remote(xs.at[i], xr.at[i], x_s.at[1 + i], x_r.at[1 + i], x_dev).wait()
    got_g = xr[0].astype(F32)
    got_u = xr[1].astype(F32)
    for i in range(2):
        g = (sums[i] + got_g[8 * i : 8 * i + 8]) * rs
        u = (sums[2 + i] + got_u[8 * i : 8 * i + 8]) * rs
        hidden_out[:, half * i : half * i + half] = (g / (1.0 + jnp.exp(-g)) * u).astype(BF16)

    def drain_dn(s):
        for i in range(4):
            dn_copy(s, i).wait_send()

    def drain_up(s):
        for i in range(4):
            up_copy(s, i).wait_send()

    loop(0, 8, drain_dn)
    loop(0, 7, drain_up)


def fused(q, kv, wo, resid, gain, gate, up, down, upf, lens, tai, pool):
    width = gate.shape[1]
    half = width // 2
    dma = pltpu.SemaphoreType.DMA
    vmem = pltpu.VMEM
    in_v = pl.BlockSpec(memory_space=pltpu.VMEM)
    in_s = pl.BlockSpec(memory_space=pltpu.SMEM)
    in_h = pl.BlockSpec(memory_space=pl.ANY)
    return pl.pallas_call(
        kernel,
        out_shape=(
            jax.ShapeDtypeStruct((ROWS, 256), BF16),
            jax.ShapeDtypeStruct((8, width), BF16),
        ),
        in_specs=[in_s] * 3 + [in_v, in_v, in_h, in_h, in_v, in_h, in_h, in_h, in_h],
        out_specs=(in_v, in_v),
        scratch_shapes=[
            vmem((2, 272, 128), BF16),
            vmem((2, 256, 256), BF16),
            vmem((16, 256), BF16),
            vmem((256, width), BF16),
            vmem((256, width), BF16),
            vmem((2, 2, RANK, width), BF16),
            vmem((8, 256, 128), BF16),
            vmem((8, 256, 128), BF16),
            vmem((8, 256, 128), BF16),
            vmem((ZS, 32, HD), BF16),
            vmem((4, 1, 128), F32),
            vmem((ZS, 32, HD), BF16),
            vmem((ZS, 1, 128), F32),
            vmem((128, 128), F32),
            vmem((ZS, 16, 256), BF16),
            vmem((32, 16, 256), BF16),
            vmem((32, 16, 256), BF16),
            vmem((NS, 16, 256), BF16),
            vmem((ZS, 16, 128), BF16),
            vmem((32, 16, 128), BF16),
            vmem((2, 1, 128), F32),
            vmem((ZS, 1, 128), F32),
            vmem((128, 128), F32),
            vmem((1, 128), F32),
            vmem((1, 128), F32),
            vmem((ROWS, width), F32),
            vmem((ROWS, width), F32),
            vmem((8, 4, 16, half), BF16),
            vmem((8, 4, 16, half), BF16),
            vmem((7, 4, 16, half), BF16),
            vmem((7, 4, 16, half), BF16),
            vmem((2, 16, half), BF16),
            vmem((2, 16, half), BF16),
            dma((6,)), dma((3,)), dma((3,)),
            dma((8,)), dma((8,)),
            dma((ZS,)), dma((ZS,)), dma((ZS,)), dma((ZS,)),
            dma((ZS,)), dma((ZS,)),
            dma((32,)), dma((32,)),
            dma((NS,)), dma((NS,)),
            dma((ZS,)), dma((ZS,)),
            dma((32,)), dma((32,)),
            dma((ZS,)), dma((ZS,)),
            dma((8, 4)), dma((8, 4)), dma((7, 4)), dma((7, 4)),
            dma((3,)), dma((3,)),
        ],
        compiler_params=pltpu.CompilerParams(
            collective_id=0, has_side_effects=True, vmem_limit_bytes=40 << 20
        ),
        cost_estimate=pl.CostEstimate(
            flops=1 << 30, bytes_accessed=1 << 23, transcendentals=1 << 18
        ),
        name="fused_layer",
    )(lens, tai, pool, q, kv, wo, resid, gain, gate, up, down, upf)


def body(
    queries,
    shared_prefix_keys,
    shared_prefix_values,
    tenant_keys,
    tenant_values,
    attention_output_weight,
    layer_residual_input,
    norm_gain_vector,
    gate_matrix,
    up_matrix,
    adapter_down_factors,
    adapter_up_factors,
    tenant_live_length,
    tenant_adapter_index,
    adapter_pool_row,
):
    x = lax.rem(lax.axis_index("wide"), 2)
    head = lax.div(lax.axis_index("narrow"), 2)
    q = lax.dynamic_slice_in_dim(queries, 2 * x, 2, 1)
    q = q.reshape(TENANTS, ROWS_T, 2, HD).transpose(0, 2, 1, 3).reshape(512, HD)

    def side(far, near):
        far = lax.dynamic_index_in_dim(far, head, 1, False)
        near = lax.dynamic_index_in_dim(near, head, 1, False)
        zero = jnp.zeros_like(near)
        return jnp.concatenate(
            [far, jnp.where(x == 0, near, zero), jnp.where(x == 0, zero, near)], axis=0
        )

    kv = jnp.stack([side(shared_prefix_keys, tenant_keys), side(shared_prefix_values, tenant_values)])
    gain = norm_gain_vector.astype(F32)[None, :]
    return fused(
        q,
        kv,
        attention_output_weight,
        layer_residual_input,
        gain,
        gate_matrix,
        up_matrix,
        adapter_down_factors,
        adapter_up_factors,
        tenant_live_length,
        tenant_adapter_index,
        adapter_pool_row,
    )


def solution(mesh):
    in_specs = (
        P(None, "narrow", None),
        P("wide", None, None),
        P("wide", None, None),
        P("wide", None, None),
        P("wide", None, None),
        P("narrow", "wide"),
        P(None, "wide"),
        P("wide"),
        P("wide", "narrow"),
        P("wide", "narrow"),
        P("narrow", "wide", None),
        P("wide", None, None, "narrow"),
        P(),
        P(),
        P(),
    )
    out_specs = (P(None, "wide"), P("wide", "narrow"))
    return jax.shard_map(body, mesh=mesh, in_specs=in_specs, out_specs=out_specs, check_vma=False)
```

time: 854 us -> 108 us (0.13)
  the two profiles are of different devices: /device:TPU:16 before, /device:TPU:2 now
where the time goes in v1:
time: 108 us
  Pallas kernels  99 us (92%)
  local copies, waits for them, and re-layouts  8.11 us (8%)
    pallas_call x1, Pallas kernels, fused(): pl.pallas_call(kernel, out_shape=(jax.ShapeDtypeStruct((ROWS, 256), BF16)...  99 us
    unnamed x27, local copies, waits for them, and re-layouts  4.86 us

profile of v1, /device:TPU:2, one launch (start us, length us, event | category | flops | bytes accessed | tf_op | source)
XLA Modules:
  0.0 108.0 jit_solution(6692859977602997161)
XLA Ops:
  0.6 0.0 copy-start
  0.7 0.0 copy-start.2
  0.7 1.6 %constant_dynamic-slice_fusion.1 = (bf16[256,1,128]{2,1,0:T(2,128)(2,1)S(1)}, bf16[256,1,128]{2,1,0:T(2,128)(2,1)S(1)}) fusion(bf16[256,8,128]{2,1,0:T(8,128)(2,1)} %param.17, s32[]{:T(128)S(6)} %select_n.44, bf16[256,8,128]{2,1,0:T(8,128)(2,1)} %param.16), kind=kLoop, calls=%fused_computation.10 | loop fusion | bytes 262148 | tf_op jit(solution)/shard_map/jit(dynamic_index_in_dim)/dynamic_slice | solution.py:499
  2.2 0.0 copy-start.1
  2.3 0.8 constant_dynamic-slice_fusion
  3.1 0.7 constant_dynamic-slice_fusion.2
  3.9 0.0 copy-done
  3.9 0.1 constant_dynamic-slice_fusion.4
  4.0 0.0 copy-start.4
  4.1 0.0 copy-start.6
  4.1 0.0 copy-start.10
  4.1 0.7 copy-done.10
  4.8 0.0 copy-start.7
  4.8 0.0 copy-start.8
  4.8 0.0 copy-start.9
  4.8 0.0 copy-done.2
  4.8 0.0 copy-done.1
  4.9 0.1 copy-done.4
  5.0 0.1 copy-done.6
  5.1 0.5 copy-done.7
  5.5 0.0 copy-done.8
  5.5 0.0 copy-done.9
  5.6 0.0 copy-start.3
  5.6 1.2 %copy-done.3 = bf16[2,2,64,1792]{3,2,1,0:T(8,128)(2,1)S(1)} copy-done((bf16[2,2,64,1792]{3,2,1,0:T(8,128)(2,1)S(1)}, bf16[2,2,64,1792]{3,2,1,0:T(8,128)(2,1)}, u32[]{:S(2)}) %copy-start.3) | copy-done | bytes 917528
  6.7 0.0 copy-start.5
  6.7 0.9 copy-done.5
  7.7 99.0 %fused_layer.1 = (bf16[256,256]{1,0:T(8,128)(2,1)S(1)}, bf16[8,1792]{1,0:T(8,128)(2,1)S(1)}) custom-call(s32[16]{0:T(128)S(1)} %copy-done.7, s32[16]{0:T(128)S(1)} %copy-done.8, s32[64]{0:T(128)S(1)} %copy-done.9, bf16[512,128]{1,0:T(8,128)(2,1)S(1)} %bitcast.23, bf16[2,272,128]{2,1,0:T(8,128)(2,1)S(1)} %pad_maximum_fusion.kv, ...), custom_call_target="tpu_custom_call" | custom-call | flops 1073741824 | bytes 8388608 | tf_op jit(solution)/shard_map/fused_layer/pallas_call | solution.py:412
  106.7 0.7 copy.40
  107.4 0.6 copy.41
  (9 shorter events, 0.1 us)
Async XLA Ops:
  0.6 3.3 %copy-start = (bf16[256,4,128]{2,1,0:T(4,128)(2,1)S(1)}, bf16[256,4,128]{2,1,0:T(4,128)(2,1)}, u32[]{:S(2)}) copy-start(bf16[256,4,128]{2,1,0:T(4,128)(2,1)} %param.15) | copy-start | bytes 786436
  0.7 4.2 %copy-start.2 = (bf16[256,1792]{1,0:T(8,128)(2,1)S(1)}, bf16[256,1792]{1,0:T(8,128)(2,1)}, u32[]{:S(2)}) copy-start(bf16[256,1792]{1,0:T(8,128)(2,1)} %up.1) | copy-start | bytes 2752516
  2.2 2.6 %copy-start.1 = (bf16[256,1792]{1,0:T(8,128)(2,1)S(1)}, bf16[256,1792]{1,0:T(8,128)(2,1)}, u32[]{:S(2)}) copy-start(bf16[256,1792]{1,0:T(8,128)(2,1)} %gate.1) | copy-start | bytes 2752516
  4.0 1.0 copy-start.4
  4.1 1.0 copy-start.6
  4.1 0.7 copy-start.10
  4.8 0.7 copy-start.7
  4.8 0.7 copy-start.8
  4.8 0.7 copy-start.9
  5.6 1.2 %copy-start.3 = (bf16[2,2,64,1792]{3,2,1,0:T(8,128)(2,1)S(1)}, bf16[2,2,64,1792]{3,2,1,0:T(8,128)(2,1)}, u32[]{:S(2)}) copy-start(bf16[2,2,64,1792]{3,2,1,0:T(8,128)(2,1)} %upf.1) | copy-start | bytes 2752516
  6.7 0.9 copy-start.5

commit v2 on v1

v2 whole, which is shorter than its diff:
```python
import jax
import jax.numpy as jnp
from jax import lax
from jax.experimental import pallas as pl
from jax.experimental.pallas import tpu as pltpu
from jax.sharding import PartitionSpec as P

MODEL_WIDTH = 8192
RANK = 64
TENANTS = 16
ROWS_T = 16
ROWS = 256
HD = 128
ZS = 16
NS = 16
NEAR = 16
MESH = pl.DeviceIdType.MESH
F32 = jnp.float32
BF16 = jnp.bfloat16


def dot(a, b):
    return jnp.dot(a, b, preferred_element_type=F32)


def dot_t(a, b):
    return lax.dot_general(a, b, (((1,), (1,)), ((), ())), preferred_element_type=F32)


def kernel(
    lens, tai, pool, q, far_k, far_v, kvn, wo, resid, gain, gate, up, down, upf,
    stream_out, hidden_out,
    kv, kvp, raw, wbuf, rbuf, gfull, ufull, ffull, down8, dsend, drecv,
    obuf, lse_s, arecv, lrecv, lt, attbuf, cbuf, crecv, sbuf,
    low_x, low_y, low_z, low_n, ss_s, ss_r, sst, ss_x, ss_y, pg, pu,
    dn_s, dn_r, up_s, up_r, xs, xr,
    loc_sem, one_s, one_r, send_sem, recv_sem, dns_sem, dnr_sem, ups_sem, upr_sem,
):
    w = lax.axis_index("wide")
    n = lax.axis_index("narrow")
    z, x = lax.div(w, 2), lax.rem(w, 2)
    chip, core = lax.div(n, 2), lax.rem(n, 2)
    ox = 1 - x
    half = gate.shape[1] // 2

    def zdev(j):
        return (j * 2 + x, n)

    def pdev(j):
        return (z * 2 + lax.div(j, NS), lax.rem(j, NS))

    me_p = x * NS + n
    x_dev = (z * 2 + ox, n)
    core_dev = (w, chip * 2 + 1 - core)

    def remote(src, dst, ss, rs, dev):
        return pltpu.make_async_remote_copy(
            src_ref=src, dst_ref=dst, send_sem=ss, recv_sem=rs, device_id=dev, device_id_type=MESH
        )

    def loop(lo, hi, fn):
        def step(i, carry):
            fn(i)
            return carry

        lax.fori_loop(lo, hi, step, 0)

    def phase(i, src, dst, dev):
        return remote(src, dst, send_sem.at[i], recv_sem.at[i], dev)

    def whole(i, src, dst):
        return phase(i, src, dst, x_dev)

    core_rows = pl.ds(pl.multiple_of(core * 4, 4), 4)

    raw_copies = [
        pltpu.make_async_copy(ref, raw.at[i], loc_sem.at[6 + i]) for i, ref in enumerate((far_k, far_v))
    ]
    for c in raw_copies:
        c.start()
    local = [
        pltpu.make_async_copy(wo.at[pl.ds(pl.multiple_of(x * 256, 256), 256)], wbuf.at[x], loc_sem.at[0]),
        pltpu.make_async_copy(resid.at[pl.ds(pl.multiple_of(n * 16, 16), 16)], rbuf, loc_sem.at[1]),
        pltpu.make_async_copy(down, down8.at[core_rows], loc_sem.at[2]),
        pltpu.make_async_copy(gate, gfull, loc_sem.at[3]),
        pltpu.make_async_copy(up, ufull, loc_sem.at[4]),
        pltpu.make_async_copy(upf, ffull, loc_sem.at[5]),
    ]
    for c in local:
        c.start()

    barrier = pltpu.get_barrier_semaphore()

    def greet_z(k):
        pl.semaphore_signal(barrier, inc=1, device_id=zdev(lax.rem(z + k, ZS)), device_id_type=MESH)

    def greet_p(k):
        pl.semaphore_signal(barrier, inc=1, device_id=pdev(lax.rem(me_p + k, 32)), device_id_type=MESH)

    loop(1, ZS, greet_z)
    loop(1, 32, greet_p)

    head = lax.broadcasted_iota(jnp.int32, (256, 8, HD), 1)
    for i in range(2):
        raw_copies[i].wait()
        kv[i, :256] = jnp.sum(jnp.where(head == chip, raw[i].astype(F32), 0.0), axis=1).astype(BF16)
        kv[i, 256:272] = kvn[i]
    pl.semaphore_wait(barrier, ZS - 1 + 31)

    kv_copy = remote(kv, kvp, one_s.at[0], one_r.at[0], x_dev)
    kv_copy.start()
    down_copy = remote(down, down8.at[core_rows], one_s.at[1], one_r.at[1], core_dev)
    down_copy.start()

    wo_copy = remote(
        wo.at[pl.ds(pl.multiple_of(ox * 256, 256), 256)], wbuf.at[x], one_s.at[2], one_r.at[2], x_dev
    )
    wo_copy.start()

    scale = HD ** (-0.5)
    qv = q[...]
    s_a = dot_t(qv, kv[0, :256]) * scale
    kv_copy.wait()
    s_b = dot_t(qv, kvp[0, :256]) * scale
    m = jnp.maximum(jnp.max(s_a, axis=1, keepdims=True), jnp.max(s_b, axis=1, keepdims=True))
    p_a = jnp.exp(s_a - m)
    p_b = jnp.exp(s_b - m)
    l = jnp.sum(p_a, axis=1, keepdims=True) + jnp.sum(p_b, axis=1, keepdims=True)
    o = dot(p_a.astype(BF16), kv[1, :256]) + dot(p_b.astype(BF16), kvp[1, :256])
    o = o / l
    lse = m + jnp.log(l)
    obuf[...] = o.astype(BF16).reshape(ZS, 32, HD)
    lse_rows = jnp.transpose(jnp.broadcast_to(lse, (512, 128)))
    for i in range(4):
        lse_s[i] = lse_rows[0:1, 128 * i : 128 * i + 128]

    def send_a(k):
        j = lax.rem(z + k, ZS)
        phase(0, obuf.at[j], arecv.at[z], zdev(j)).start()
        phase(1, lse_s.at[lax.div(j, 4)], lrecv.at[z], zdev(j)).start()

    loop(1, ZS, send_a)

    local[2].wait()
    down_copy.wait()

    def pick(i):
        slot = pool[tai[2 * i + core]]
        block = down8[lax.rem(slot, 8)]
        mine = lax.div(slot, 8) == chip
        dsend[i] = jnp.where(mine, block, jnp.zeros_like(block))

    loop(0, 8, pick)

    def send_down(k):
        j = lax.rem(chip + k, 8)
        phase(2, dsend.at[j], drecv.at[chip], (w, j * 2 + core)).start()

    loop(1, 5, send_down)

    nk = kv[0, 256:272] + kvp[0, 256:272]
    nv = kv[1, 256:272] + kvp[1, 256:272]
    q_own = q[pl.ds(pl.multiple_of(z * 32, 32), 32), :]
    near = dot_t(q_own, nk) * scale
    row = lax.rem(lax.broadcasted_iota(jnp.int32, (32, NEAR), 0), ROWS_T)
    col = lax.broadcasted_iota(jnp.int32, (32, NEAR), 1)
    ok = (col <= row) & (col < lens[z])
    near = jnp.where(ok, near, -jnp.inf)
    m_n = jnp.max(near, axis=1, keepdims=True)
    p_n = jnp.where(ok, jnp.exp(near - m_n), 0.0)
    l_n = jnp.sum(p_n, axis=1, keepdims=True)
    o_n = dot(p_n.astype(BF16), nv) / l_n
    lse_n = m_n + jnp.log(l_n)
    drecv[chip] = dsend[chip]
    arecv[z] = obuf[z]
    lrecv[z] = lse_s[lax.div(z, 4)]

    whole(1, lrecv.at[pl.ds(0, ZS - 1)], lrecv.at[pl.ds(0, ZS - 1)]).wait_recv()
    rows16 = jnp.concatenate([lrecv[s] for s in range(ZS)], axis=0)
    lt[...] = jnp.transpose(jnp.concatenate([rows16] * 8, axis=0))
    cols = lt[pl.ds(pl.multiple_of(lax.rem(z, 4) * 32, 32), 32), :]
    top = jnp.maximum(jnp.max(cols, axis=1, keepdims=True), lse_n)
    part = jnp.exp(cols - top)
    w_n = jnp.exp(lse_n - top)
    lane = lax.broadcasted_iota(jnp.int32, (32, 128), 1)
    total = jnp.sum(jnp.where(lane < ZS, part, 0.0), axis=1, keepdims=True) + w_n
    acc = w_n * o_n
    whole(0, arecv.at[pl.ds(0, ZS - 1)], arecv.at[pl.ds(0, ZS - 1)]).wait_recv()
    for s in range(ZS):
        acc = acc + part[:, s : s + 1] * arecv[s].astype(F32)
    acc = acc / total
    attbuf[z] = jnp.concatenate([acc[:16], acc[16:]], axis=1).astype(BF16)

    def send_b(k):
        j = lax.rem(z + k, ZS)
        phase(3, attbuf.at[z], attbuf.at[z], zdev(j)).start()

    loop(1, ZS, send_b)
    loop(5, 8, send_down)
    local[0].wait()
    wo_copy.wait()
    whole(3, attbuf.at[pl.ds(0, ZS - 1)], attbuf.at[pl.ds(0, ZS - 1)]).wait_recv()
    att = attbuf[...].reshape(ROWS, 256)
    for xf in range(2):
        cbuf[pl.ds(xf * NS, NS)] = dot(att, wbuf[xf]).astype(BF16).reshape(NS, 16, 256)

    def send_c(k):
        j = lax.rem(me_p + k, 32)
        phase(4, cbuf.at[j], crecv.at[me_p], pdev(j)).start()

    loop(1, 32, send_c)
    crecv[me_p] = cbuf[me_p]
    local[1].wait()
    whole(2, drecv.at[pl.ds(0, 7)], drecv.at[pl.ds(0, 7)]).wait_recv()
    dsel = drecv[0].astype(F32)
    for i in range(1, 8):
        dsel = dsel + drecv[i].astype(F32)
    dsel = dsel.astype(BF16)
    pos = lax.broadcasted_iota(jnp.int32, (16, 256), 0)
    gain_row = gain[...]
    whole(4, crecv.at[pl.ds(0, 31)], crecv.at[pl.ds(0, 31)]).wait_recv()
    acc = rbuf[...].astype(F32)
    for s in range(32):
        acc = acc + crecv[s].astype(F32)
    mine = jnp.where(pos < lens[n], acc, 0.0).astype(BF16)
    sbuf[n] = mine

    low_x[...] = dot((mine.astype(F32) * gain_row).astype(BF16), dsel)
    lx_copy = remote(low_x, low_y, one_s.at[7], one_r.at[7], x_dev)
    lx_copy.start()

    def send_e(k):
        j = lax.rem(n + k, NS)
        phase(5, sbuf.at[n], sbuf.at[n], (w, j)).start()

    loop(1, NS, send_e)
    lx_copy.wait()
    low_z[z] = (low_x[...] + low_y[...]).astype(BF16)

    def send_lz(k):
        j = lax.rem(z + k, ZS)
        phase(6, low_z.at[z], low_z.at[z], zdev(j)).start()

    loop(1, ZS, send_lz)

    whole(5, sbuf.at[pl.ds(0, NS - 1)], sbuf.at[pl.ds(0, NS - 1)]).wait_recv()
    stream = sbuf[...].reshape(ROWS, 256)
    stream_out[...] = stream
    sf = stream.astype(F32)
    ssq = jnp.sum(sf * sf, axis=1, keepdims=True)
    y = (sf * gain_row).astype(BF16)

    whole(6, low_z.at[pl.ds(0, ZS - 1)], low_z.at[pl.ds(0, ZS - 1)]).wait_recv()
    acc = low_z[0].astype(F32)
    for s in range(1, ZS):
        acc = acc + low_z[s].astype(F32)
    low_n[n] = acc.astype(BF16)

    def send_lp(k):
        j = lax.rem(n + k, NS)
        phase(7, low_n.at[n], low_n.at[n], (w, j)).start()

    loop(1, NS, send_lp)

    local[3].wait()
    pg[...] = dot(y, gfull[...])
    local[4].wait()
    local[5].wait()
    ss_rows = jnp.transpose(jnp.broadcast_to(ssq, (ROWS, 128)))
    for i in range(2):
        ss_s[i] = ss_rows[0:1, 128 * i : 128 * i + 128]
    smap = jnp.concatenate(
        [jnp.full((ROWS_T, 128), pool[tai[t]], jnp.int32) for t in range(TENANTS)], axis=0
    )
    lane2 = lax.broadcasted_iota(jnp.int32, (ROWS, 128), 1)
    first = lane2 < RANK

    whole(7, low_n.at[pl.ds(0, NS - 1)], low_n.at[pl.ds(0, NS - 1)]).wait_recv()
    lows = low_n[...].astype(F32).reshape(ROWS, 128)
    rolled = pltpu.roll(lows, RANK, 1)
    owned = smap == (2 * w + jnp.where(first, 0, 1))
    l_gate = jnp.where(owned, jnp.where(first, lows, rolled), 0.0).astype(BF16)
    l_up = jnp.where(owned, jnp.where(first, rolled, lows), 0.0).astype(BF16)

    def rank_part(i):
        side, cols = i // 2, slice(half * (i % 2), half * (i % 2) + half)
        factors = jnp.concatenate([ffull[0, side, :, cols], ffull[1, side, :, cols]], axis=0)
        if side == 0:
            pg[:, cols] += dot(l_gate, factors)
        else:
            pu[:, cols] = dot(y, ufull[:, cols]) + dot(l_up, factors)

    below, above = lax.rem(z + ZS - 1, ZS), lax.rem(z + 1, ZS)
    parts = [(pg, 0), (pg, half), (pu, 0), (pu, half)]

    def own_rows(i, t):
        ref, at = parts[i]
        return ref[pl.ds(pl.multiple_of(t * 16, 16), 16), at : at + half]

    def dn_copy(s, i):
        return remote(dn_s.at[s, i], dn_r.at[s, i], dns_sem.at[s, i], dnr_sem.at[s, i], zdev(below))

    def up_copy(s, i):
        return remote(up_s.at[s, i], up_r.at[s, i], ups_sem.at[s, i], upr_sem.at[s, i], zdev(above))

    def send_ss(k):
        j = lax.rem(z + k, ZS)
        phase(8, ss_s.at[lax.div(j, 8)], ss_r.at[z], zdev(j)).start()

    for i in range(4):
        rank_part(i)
        dn_s[0, i] = own_rows(i, lax.rem(z + 8, ZS)).astype(BF16)
        dn_copy(0, i).start()
        up_s[0, i] = own_rows(i, lax.rem(z + 7, ZS)).astype(BF16)
        up_copy(0, i).start()
        if i == 1:
            loop(1, ZS, send_ss)

    def ring(s):
        for i in range(4):
            dn_copy(s - 1, i).wait_recv()
            got = dn_r[s - 1, i].astype(F32) + own_rows(i, lax.rem(z + 8 + s, ZS))
            dn_s[s, i] = got.astype(BF16)
            dn_copy(s, i).start()
            up_copy(s - 1, i).wait_recv()
            got = up_r[s - 1, i].astype(F32) + own_rows(i, lax.rem(z + 7 - s + ZS, ZS))
            up_s[s, i] = got.astype(BF16)
            up_copy(s, i).start()

    ss_r[z] = ss_s[lax.div(z, 8)]
    loop(1, 7, ring)
    for i in range(4):
        dn_copy(6, i).wait_recv()
        got = dn_r[6, i].astype(F32) + own_rows(i, lax.rem(z + 15, ZS))
        dn_s[7, i] = got.astype(BF16)
        dn_copy(7, i).start()

    whole(8, ss_r.at[pl.ds(0, ZS - 1)], ss_r.at[pl.ds(0, ZS - 1)]).wait_recv()
    acc = ss_r[0]
    for s in range(1, ZS):
        acc = acc + ss_r[s]
    ss_x[...] = acc
    ss_copy = remote(ss_x, ss_y, one_s.at[3], one_r.at[3], x_dev)
    ss_copy.start()

    sums = []
    for i in range(4):
        up_copy(6, i).wait_recv()
        part_sum = own_rows(i, z) + up_r[6, i].astype(F32)
        dn_copy(7, i).wait_recv()
        part_sum = part_sum + dn_r[7, i].astype(F32)
        other = jnp.where(x == 0, part_sum[8:], part_sum[:8])
        xs_rows = other
        sums.append(jnp.where(x == 0, part_sum[:8], part_sum[8:]))
        if i % 2 == 0:
            held = xs_rows
        else:
            xs[i // 2] = jnp.concatenate([held, xs_rows], axis=0).astype(BF16)
            remote(xs.at[i // 2], xr.at[i // 2], one_s.at[4 + i // 2], one_r.at[4 + i // 2], x_dev).start()

    ss_copy.wait()
    squares = ss_x[...] + ss_y[...]
    sst[...] = jnp.transpose(jnp.broadcast_to(squares, (128, 128)))
    own_sq = sst[pl.ds(pl.multiple_of(lax.rem(z, 8) * 16 + x * 8, 8), 8), 0:1]
    rs = lax.rsqrt(own_sq / MODEL_WIDTH + 1e-05)
    for i in range(2):
        remote(xs.at[i], xr.at[i], one_s.at[4 + i], one_r.at[4 + i], x_dev).wait()
    got_g = xr[0].astype(F32)
    got_u = xr[1].astype(F32)
    for i in range(2):
        g = (sums[i] + got_g[8 * i : 8 * i + 8]) * rs
        u = (sums[2 + i] + got_u[8 * i : 8 * i + 8]) * rs
        hidden_out[:, half * i : half * i + half] = (g / (1.0 + jnp.exp(-g)) * u).astype(BF16)

    def drain_dn(s):
        for i in range(4):
            dn_copy(s, i).wait_send()

    def drain_up(s):
        for i in range(4):
            up_copy(s, i).wait_send()

    loop(0, 8, drain_dn)
    loop(0, 7, drain_up)
    for i, ref in (
        (0, arecv.at[pl.ds(0, 15)]), (1, lrecv.at[pl.ds(0, 15)]), (2, drecv.at[pl.ds(0, 7)]),
        (3, attbuf.at[pl.ds(0, 15)]), (4, crecv.at[pl.ds(0, 31)]), (5, sbuf.at[pl.ds(0, 15)]),
        (6, low_z.at[pl.ds(0, 15)]), (7, low_n.at[pl.ds(0, 15)]), (8, ss_r.at[pl.ds(0, 15)]),
    ):
        whole(i, ref, ref).wait_send()


def fused(q, far_k, far_v, kvn, wo, resid, gain, gate, up, down, upf, lens, tai, pool):
    width = gate.shape[1]
    half = width // 2
    dma = pltpu.SemaphoreType.DMA
    vmem = pltpu.VMEM
    in_v = pl.BlockSpec(memory_space=pltpu.VMEM)
    in_s = pl.BlockSpec(memory_space=pltpu.SMEM)
    in_h = pl.BlockSpec(memory_space=pl.ANY)
    return pl.pallas_call(
        kernel,
        out_shape=(
            jax.ShapeDtypeStruct((ROWS, 256), BF16),
            jax.ShapeDtypeStruct((8, width), BF16),
        ),
        in_specs=[in_s] * 3 + [in_v, in_h, in_h, in_v, in_h, in_h, in_v, in_h, in_h, in_h, in_h],
        out_specs=(in_v, in_v),
        scratch_shapes=[
            vmem((2, 272, 128), BF16),
            vmem((2, 272, 128), BF16),
            vmem((2, 256, 8, 128), BF16),
            vmem((2, 256, 256), BF16),
            vmem((16, 256), BF16),
            vmem((256, width), BF16),
            vmem((256, width), BF16),
            vmem((2, 2, RANK, width), BF16),
            vmem((8, 256, 128), BF16),
            vmem((8, 256, 128), BF16),
            vmem((8, 256, 128), BF16),
            vmem((ZS, 32, HD), BF16),
            vmem((4, 1, 128), F32),
            vmem((ZS, 32, HD), BF16),
            vmem((ZS, 1, 128), F32),
            vmem((128, 128), F32),
            vmem((ZS, 16, 256), BF16),
            vmem((32, 16, 256), BF16),
            vmem((32, 16, 256), BF16),
            vmem((NS, 16, 256), BF16),
            vmem((16, 128), F32),
            vmem((16, 128), F32),
            vmem((ZS, 16, 128), BF16),
            vmem((NS, 16, 128), BF16),
            vmem((2, 1, 128), F32),
            vmem((ZS, 1, 128), F32),
            vmem((128, 128), F32),
            vmem((1, 128), F32),
            vmem((1, 128), F32),
            vmem((ROWS, width), F32),
            vmem((ROWS, width), F32),
            vmem((8, 4, 16, half), BF16),
            vmem((8, 4, 16, half), BF16),
            vmem((7, 4, 16, half), BF16),
            vmem((7, 4, 16, half), BF16),
            vmem((2, 16, half), BF16),
            vmem((2, 16, half), BF16),
            dma((8,)), dma((9,)), dma((9,)), dma((9,)), dma((9,)),
            dma((8, 4)), dma((8, 4)), dma((7, 4)), dma((7, 4)),
        ],
        compiler_params=pltpu.CompilerParams(
            collective_id=0, has_side_effects=True, vmem_limit_bytes=60 << 20
        ),
        cost_estimate=pl.CostEstimate(
            flops=1 << 30, bytes_accessed=1 << 23, transcendentals=1 << 18
        ),
        name="fused_layer",
    )(lens, tai, pool, q, far_k, far_v, kvn, wo, resid, gain, gate, up, down, upf)


def body(
    queries,
    shared_prefix_keys,
    shared_prefix_values,
    tenant_keys,
    tenant_values,
    attention_output_weight,
    layer_residual_input,
    norm_gain_vector,
    gate_matrix,
    up_matrix,
    adapter_down_factors,
    adapter_up_factors,
    tenant_live_length,
    tenant_adapter_index,
    adapter_pool_row,
):
    x = lax.rem(lax.axis_index("wide"), 2)
    head = lax.div(lax.axis_index("narrow"), 2)
    q = lax.dynamic_slice_in_dim(queries, 2 * x, 2, 1)
    q = q.reshape(TENANTS, ROWS_T, 2, HD).transpose(0, 2, 1, 3).reshape(512, HD)

    def side(near):
        near = lax.dynamic_index_in_dim(near, head, 1, False)
        zero = jnp.zeros_like(near)
        return jnp.concatenate([jnp.where(x == 0, near, zero), jnp.where(x == 0, zero, near)], axis=0)

    kvn = jnp.stack([side(tenant_keys), side(tenant_values)])
    gain = norm_gain_vector.astype(F32)[None, :]
    return fused(
        q,
        shared_prefix_keys,
        shared_prefix_values,
        kvn,
        attention_output_weight,
        layer_residual_input,
        gain,
        gate_matrix,
        up_matrix,
        adapter_down_factors,
        adapter_up_factors,
        tenant_live_length,
        tenant_adapter_index,
        adapter_pool_row,
    )


def solution(mesh):
    in_specs = (
        P(None, "narrow", None),
        P("wide", None, None),
        P("wide", None, None),
        P("wide", None, None),
        P("wide", None, None),
        P("narrow", "wide"),
        P(None, "wide"),
        P("wide"),
        P("wide", "narrow"),
        P("wide", "narrow"),
        P("narrow", "wide", None),
        P("wide", None, None, "narrow"),
        P(),
        P(),
        P(),
    )
    out_specs = (P(None, "wide"), P("wide", "narrow"))
    return jax.shard_map(body, mesh=mesh, in_specs=in_specs, out_specs=out_specs, check_vma=False)
```

time: 108 us -> 105 us (0.972)
  local copies, waits for them, and re-layouts: 8.11 us -> 5.15 us
  other arithmetic: 0.04 us -> 1.17 us
    unnamed x27 -> x9, local copies, waits for them, and re-layouts: 4.86 us -> 2.9 us
    dynamic_slice x1 -> x0, local copies, waits for them, and re-layouts: 1.57 us -> none  [side(): far = lax.dynamic_index_in_dim(far, head, 1, False)]
where the time goes in v2:
time: 105 us
  Pallas kernels  98.1 us (93%)
  local copies, waits for them, and re-layouts  5.15 us (5%)
  other arithmetic  1.17 us (1%)
    pallas_call x1, Pallas kernels, fused(): pl.pallas_call(kernel, out_shape=(jax.ShapeDtypeStruct((ROWS, 256), BF16)...  98.1 us
    unnamed x9, local copies, waits for them, and re-layouts  2.9 us

profile of v2, /device:TPU:2, one launch (start us, length us, event | category | flops | bytes accessed | tf_op | source)
XLA Modules:
  0.0 105.2 jit_solution(14116647120077878300)
XLA Ops:
  0.6 0.0 copy-start
  0.7 0.0 copy-start.2
  0.7 0.7 copy-done.2
  1.4 0.5 broadcast_in_dim.7
  1.9 0.7 constant_dynamic-slice_fusion.1
  2.6 0.7 constant_dynamic-slice_fusion
  3.4 0.6 pad_maximum_fusion.kvn
  4.0 0.0 copy-done
  4.0 0.1 constant_dynamic-slice_fusion.2
  4.2 0.7 copy.20
  4.8 98.1 %fused_layer.1 = (bf16[256,256]{1,0:T(8,128)(2,1)}, bf16[8,1792]{1,0:T(8,128)(2,1)}) custom-call(s32[16]{0:T(128)} %lens.1, s32[16]{0:T(128)} %tai.1, s32[64]{0:T(128)} %pool.1, bf16[512,128]{1,0:T(8,128)(2,1)} %bitcast.17, bf16[256,8,128]{2,1,0:T(8,128)(2,1)} %far_k.1, bf16[256,8,128]{2,1,0:T(8,128)(2,1)} %far_v.1, ...), custom_call_target="tpu_custom_call" | custom-call | flops 1073741824 | bytes 8388608 | tf_op jit(solution)/shard_map/fused_layer/pallas_call | solution.py:401
  103.0 0.0 copy-start.1
  103.0 1.6 %copy.32 = bf16[256,256]{1,0:T(8,128)(2,1)} copy(bf16[256,256]{1,0:T(8,128)(2,1)} %get-tuple-element.10) | data formatting | bytes 262144
  104.5 0.0 copy-done.1
  104.5 0.6 copy.33
  (4 shorter events, 0.0 us)
Async XLA Ops:
  0.6 3.4 %copy-start = (bf16[256,4,128]{2,1,0:T(4,128)(2,1)S(1)}, bf16[256,4,128]{2,1,0:T(4,128)(2,1)}, u32[]{:S(2)}) copy-start(bf16[256,4,128]{2,1,0:T(4,128)(2,1)} %param.15) | copy-start | bytes 786436
  0.7 0.7 copy-start.2
  103.0 1.6 %copy-start.1 = (bf16[8,1792]{1,0:T(8,128)(2,1)S(1)}, bf16[8,1792]{1,0:T(8,128)(2,1)}, u32[]{:S(2)}) copy-start(bf16[8,1792]{1,0:T(8,128)(2,1)} %get-tuple-element.11) | copy-start | bytes 86020

commit v3 on v2

--- a/solution.py
+++ b/solution.py
@@ -28,9 +28,9 @@
 
 
 def kernel(
-    lens, tai, pool, q, far_k, far_v, kvn, wo, resid, gain, gate, up, down, upf,
+    lens, tai, pool, q_all, far_k, far_v, kvn, wo, resid, gain, gate, up, down, upf,
     stream_out, hidden_out,
-    kv, kvp, raw, wbuf, rbuf, gfull, ufull, ffull, down8, dsend, drecv,
+    q, kv, kvp, raw, q_raw, wbuf, rbuf, gfull, ufull, ffull, down8, dsend, drecv,
     obuf, lse_s, arecv, lrecv, lt, attbuf, cbuf, crecv, sbuf,
     low_x, low_y, low_z, low_n, ss_s, ss_r, sst, ss_x, ss_y, pg, pu,
     dn_s, dn_r, up_s, up_r, xs, xr,
@@ -76,6 +76,7 @@
     raw_copies = [
         pltpu.make_async_copy(ref, raw.at[i], loc_sem.at[6 + i]) for i, ref in enumerate((far_k, far_v))
     ]
+    raw_copies.append(pltpu.make_async_copy(q_all, q_raw, loc_sem.at[8]))
     for c in raw_copies:
         c.start()
     local = [
@@ -105,6 +106,13 @@
         raw_copies[i].wait()
         kv[i, :256] = jnp.sum(jnp.where(head == chip, raw[i].astype(F32), 0.0), axis=1).astype(BF16)
         kv[i, 256:272] = kvn[i]
+    raw_copies[2].wait()
+    which = lax.broadcasted_iota(jnp.int32, (256, 4, HD), 1)
+    qf = q_raw[...].astype(F32)
+    picked = [
+        jnp.sum(jnp.where(which == 2 * x + h, qf, 0.0), axis=1).reshape(TENANTS, ROWS_T, HD) for h in range(2)
+    ]
+    q[...] = jnp.concatenate(picked, axis=1).reshape(512, HD).astype(BF16)
     pl.semaphore_wait(barrier, ZS - 1 + 31)
 
     kv_copy = remote(kv, kvp, one_s.at[0], one_r.at[0], x_dev)
@@ -404,12 +412,14 @@
             jax.ShapeDtypeStruct((ROWS, 256), BF16),
             jax.ShapeDtypeStruct((8, width), BF16),
         ),
-        in_specs=[in_s] * 3 + [in_v, in_h, in_h, in_v, in_h, in_h, in_v, in_h, in_h, in_h, in_h],
+        in_specs=[in_s] * 3 + [in_h, in_h, in_h, in_v, in_h, in_h, in_v, in_h, in_h, in_h, in_h],
         out_specs=(in_v, in_v),
         scratch_shapes=[
+            vmem((512, HD), BF16),
             vmem((2, 272, 128), BF16),
             vmem((2, 272, 128), BF16),
             vmem((2, 256, 8, 128), BF16),
+            vmem((256, 4, HD), BF16),
             vmem((2, 256, 256), BF16),
             vmem((16, 256), BF16),
             vmem((256, width), BF16),
@@ -444,7 +454,7 @@
             vmem((7, 4, 16, half), BF16),
             vmem((2, 16, half), BF16),
             vmem((2, 16, half), BF16),
-            dma((8,)), dma((9,)), dma((9,)), dma((9,)), dma((9,)),
+            dma((9,)), dma((9,)), dma((9,)), dma((9,)), dma((9,)),
             dma((8, 4)), dma((8, 4)), dma((7, 4)), dma((7, 4)),
         ],
         compiler_params=pltpu.CompilerParams(
@@ -476,8 +486,6 @@
 ):
     x = lax.rem(lax.axis_index("wide"), 2)
     head = lax.div(lax.axis_index("narrow"), 2)
-    q = lax.dynamic_slice_in_dim(queries, 2 * x, 2, 1)
-    q = q.reshape(TENANTS, ROWS_T, 2, HD).transpose(0, 2, 1, 3).reshape(512, HD)
 
     def side(near):
         near = lax.dynamic_index_in_dim(near, head, 1, False)
@@ -487,7 +495,7 @@
     kvn = jnp.stack([side(tenant_keys), side(tenant_values)])
     gain = norm_gain_vector.astype(F32)[None, :]
     return fused(
-        q,
+        queries,
         shared_prefix_keys,
         shared_prefix_values,
         kvn,

time: 105 us -> 103 us (0.981)
  the two profiles are of different devices: /device:TPU:2 before, /device:TPU:4 now
where the time goes in v3:
time: 103 us
  Pallas kernels  97.7 us (95%)
  local copies, waits for them, and re-layouts  3.58 us (3%)
  other arithmetic  1.18 us (1%)
    pallas_call x1, Pallas kernels, fused(): pl.pallas_call(kernel, out_shape=(jax.ShapeDtypeStruct((ROWS, 256), BF16)...  97.7 us
    unnamed x8, local copies, waits for them, and re-layouts  2.84 us

profile of v3, /device:TPU:4, one launch (start us, length us, event | category | flops | bytes accessed | tf_op | source)
XLA Modules:
  0.0 103.2 jit_solution(18429929857568065386)
XLA Ops:
  0.6 0.0 copy-start
  0.7 0.0 copy-start.2
  0.7 0.6 copy-done.2
  1.3 0.6 broadcast_in_dim.7
  1.9 0.0 copy-done
  1.9 0.7 constant_dynamic-slice_fusion
  2.7 0.6 pad_maximum_fusion.kvn
  3.3 97.7 %fused_layer.1 = (bf16[256,256]{1,0:T(8,128)(2,1)}, bf16[8,1792]{1,0:T(8,128)(2,1)}) custom-call(s32[16]{0:T(128)} %lens.1, s32[16]{0:T(128)} %tai.1, s32[64]{0:T(128)} %pool.1, bf16[256,4,128]{2,1,0:T(4,128)(2,1)} %q_all.1, bf16[256,8,128]{2,1,0:T(8,128)(2,1)} %far_k.1, bf16[256,8,128]{2,1,0:T(8,128)(2,1)} %far_v.1, ...), custom_call_target="tpu_custom_call" | custom-call | flops 1073741824 | bytes 8388608 | tf_op jit(solution)/shard_map/fused_layer/pallas_call | solution.py:409
  101.0 0.0 copy-start.1
  101.0 1.6 %copy.27 = bf16[256,256]{1,0:T(8,128)(2,1)} copy(bf16[256,256]{1,0:T(8,128)(2,1)} %get-tuple-element.10) | data formatting | bytes 262144
  102.6 0.0 copy-done.1
  102.6 0.6 copy.28
  (4 shorter events, 0.0 us)
Async XLA Ops:
  0.6 1.2 %copy-start = (bf16[8,8,128]{2,1,0:T(8,128)(2,1)S(1)}, bf16[8,8,128]{2,1,0:T(8,128)(2,1)}, u32[]{:S(2)}) copy-start(bf16[8,8,128]{2,1,0:T(8,128)(2,1)} %param.18) | copy-start | bytes 49156
  0.7 0.7 copy-start.2
  101.0 1.6 %copy-start.1 = (bf16[8,1792]{1,0:T(8,128)(2,1)S(1)}, bf16[8,1792]{1,0:T(8,128)(2,1)}, u32[]{:S(2)}) copy-start(bf16[8,1792]{1,0:T(8,128)(2,1)} %get-tuple-element.11) | copy-start | bytes 86020
